TPU v7x, 512 devices: a whole 4x4x16 slice. The times are simulated.
512 devices in a mesh: row: 32 (over z, x_lo), col: 16 (over x_hi, y, core).
Axes of the slice: x: 4 (x_hi: 2, x_lo: 2; x = x_hi * 2 + x_lo), y: 4, z: 16, core: 2. Of those that a mesh axis runs over, the one named last changes fastest.
Arguments:
- spectra: float32 [2, 2, 512, 10240], P(None, None, 'row', 'col'), may hold values from -6 to 6
Outputs:
- cross_spectra: float32 [2, 2, 10240, 10240], P(None, None, 'row', 'col')
All inputs are finite; a program needn't handle non-finite values.
Results may differ from a plain program's by a relative error of at most 0.000094.
Values sent between devices are 32-bit elements; how exact they have to be, the bound alone decides.
A program may use at most 128 MiB of HBM per device.

v0:
```python
import jax
import jax.numpy as jnp
from jax import lax
from jax.sharding import PartitionSpec as P


def broadcast(value, axis, root):
    mine = lax.axis_index(axis) == root
    return lax.psum(jnp.where(mine, value, jnp.zeros_like(value)), axis)


def block_products(row_panel, col_panel):
    terms = jnp.einsum(
        "fpsa,fqsb->fpqab",
        row_panel,
        col_panel,
        precision=lax.Precision.HIGHEST,
        preferred_element_type=jnp.float32,
    )
    real_out = terms[:, 0, 0] + terms[:, 1, 1]
    imag_out = terms[:, 1, 0] - terms[:, 0, 1]
    return jnp.stack([real_out, imag_out], axis=1)


def collect_panels(shard_part):
    col_panel = lax.all_gather(shard_part, "row", axis=2, tiled=True)
    row_ratio = lax.axis_size("row") // lax.axis_size("col")
    row_width = shard_part.shape[3] // row_ratio
    row_number = lax.axis_index("row")
    row_slice = lax.dynamic_slice_in_dim(
        col_panel, row_number % row_ratio * row_width, row_width, 3
    )
    row_panel = broadcast(row_slice, "col", row_number // row_ratio)
    return (row_panel, col_panel)


def per_device(spectra):
    segment_total = float(spectra.shape[2] * lax.axis_size("row"))
    row_panel, col_panel = collect_panels(spectra)
    segment_sums = block_products(row_panel, col_panel)
    return segment_sums / segment_total


def solution(mesh):
    return jax.shard_map(
        per_device,
        mesh=mesh,
        in_specs=(P(None, None, "row", "col"),),
        out_specs=P(None, None, "row", "col"),
        check_vma=False,
    )
```

profile of v0, /device:TPU:1, one launch (start us, length us, event | category | flops | bytes accessed | tf_op | source)
XLA Modules:
  0.0 348.9 jit_solution(6011433992663984414)
XLA Ops:
  6.5 0.0 all-gather.2.cloned.1.call-start
  6.5 0.7 all-gather.2.cloned.1.call-update
  7.3 0.0 all-reduce.2.cloned.1.call-start
  7.3 138.4 %all-gather.2.cloned.1.call-done = f32[2,2,512,640]{3,2,1,0:T(8,128)} async-done(((f32[2,2,16,640]{3,2,1,0:T(8,128)}), f32[2,2,512,640]{3,2,1,0:T(8,128)}) %all-gather.2.cloned.1.call-update) | async-done | bytes 5242896 | tf_op jit(solution)/shard_map/all_gather | solution.py:26
  145.7 4.7 %dynamic-slice_select_fusion = f32[2,2,512,320]{3,2,1,0:T(8,128)} fusion(f32[2,2,512,640]{3,2,1,0:T(8,128)} %all-gather.2.cloned.1.call-done, s32[]{:T(128)S(6)} %select_n.25, pred[]{:T(512)S(6)} %eq.5), kind=kLoop, calls=%fused_computation.4 | loop fusion | flops 655360 | bytes 5242885 | tf_op jit(solution)/shard_map/jit(_where)/select_n | solution.py:9
  150.4 0.0 all-reduce.2.cloned.1.call-update
  150.5 174.7 %all-reduce.2.cloned.1.call-done = f32[2,2,512,320]{3,2,1,0:T(8,128)} async-done(((f32[2,2,512,320]{3,2,1,0:T(8,128)}), f32[2,2,512,320]{3,2,1,0:T(8,128)}) %all-reduce.2.cloned.1.call-update) | async-done | bytes 2621456 | tf_op jit(solution)/shard_map/psum | solution.py:9
  325.2 14.4 %fusion.3 = f32[2,2,2,320,640]{4,3,2,1,0:T(8,128)S(1)} fusion(f32[2,2,512,640]{3,2,1,0:T(8,128)} %all-gather.2.cloned.1.call-done, f32[2,2,512,320]{3,2,1,0:T(8,128)} %all-reduce.2.cloned.1.call-done), kind=kOutput, calls=%fused_computation.5 | convolution fusion | flops 10066329600 | bytes 14417920 | tf_op jit(solution)/shard_map/fpsa,fqsb->fpqab/dot_general | solution.py:13
  339.6 0.2 fusion.8
  339.8 0.2 fusion.10
  339.9 0.2 maximum_multiply_fusion
  340.1 1.9 copy.5
Async XLA Ops:
  6.5 139.2 %all-gather.2.cloned.1.call-start = ((), (), s32[]{:S(2)}) async-start(), calls=%async_computation | async-start | bytes 5406720 | tf_op jit(solution)/shard_map/all_gather | solution.py:26
  7.3 317.9 %all-reduce.2.cloned.1.call-start = ((), (), s32[]{:S(2)}) async-start(), calls=%async_computation.1 | async-start | bytes 6291456 | tf_op jit(solution)/shard_map/psum | solution.py:9
Sparse Core Ops, SparseCore 0:
  9.4 136.2 all-gather.1
  150.6 174.5 all-reduce.1
where the time goes:
time: 349 us
  waiting for transfers between devices  314 us (90%)
  matrix products  14.4 us (4%)
  between operations  13.5 us (4%)
  other arithmetic  5.28 us (2%)
    psum x1, waiting for transfers between devices, broadcast(): return lax.psum(jnp.where(mine, value, jnp.zeros_like(value)), axis)  175 us
    all_gather x1, waiting for transfers between devices, collect_panels(): col_panel = lax.all_gather(shard_part, 'row', axis=2, tiled=True)  138 us
    dot_general x1, matrix products, block_products(): jnp.einsum('fpsa,fqsb->fpqab', row_panel, col_panel, precision=lax.Precis...  14.4 us
  transfers between devices with their start and end apart: 2, of which 2 were waited for; matrix products, arithmetic and copies ran while one was open for 0% of the time, Pallas kernels for 0%

commit v1 on v0

v1 whole, which is shorter than its diff:
```python
import jax
import jax.numpy as jnp
from jax import lax
from jax.experimental import pallas as pl
from jax.experimental.pallas import tpu as pltpu
from jax.sharding import PartitionSpec as P

MESH = pl.DeviceIdType.MESH
CUT = 3
WIDE = 384


def kernel(x_ref, out_ref, col, row, lhs, rhs, own_sem, zs, zr, xs, xr, rr, ups, downs, mates, nears):
    r = lax.axis_index("row")
    c = lax.axis_index("col")
    z, xl = r // 2, r % 2
    xh, y, core = c // 8, (c // 2) % 4, c % 2
    src_xh, src_y, src_core = z // 8, (z // 2) % 4, z % 2
    dy = (y - src_y + 4) % 4
    home = xh == src_xh
    is_src = home & (dy == 0) & (core == src_core)
    is_src_mate = home & (dy == 0) & (core != src_core)
    is_near = jnp.logical_not(home) & (dy == 0)
    plain = jnp.logical_not(is_src | is_src_mate)
    lag = 1 + jnp.where(home, 0, 1) + jnp.where(dy == 0, 0, 1) + jnp.where(dy == 2, 1, 0)
    lag = lag + jnp.where(is_src_mate, 1, 0)

    zdev = [((r + 2) % 32, c), ((r + 30) % 32, c)]
    xdev = (r + 1 - 2 * xl, c)
    mate = (r, c + 1 - 2 * core)

    def ydev(step, k):
        return (r, xh * 8 + ((y + step + 4) % 4) * 2 + k)

    def ndev(k):
        return (r + 1 - 2 * xl, (1 - xh) * 8 + y * 2 + k)

    own = pltpu.make_async_copy(x_ref, col.at[0], own_sem)
    own.start()
    barrier = pltpu.get_barrier_semaphore()
    greet = [zdev[0], zdev[1], xdev, mate]
    greet += [ydev(s, k) for s in (1, -1) for k in (0, 1)] + [ndev(0), ndev(1)]
    for d in greet:
        pl.semaphore_signal(barrier, inc=1, device_id=d, device_id_type=MESH)
    own.wait()
    pl.semaphore_wait(barrier, len(greet))

    A, B = pl.ds(0, CUT), pl.ds(CUT, 8 - CUT)

    def remote(src, dst, ss, rs, dev):
        return pltpu.make_async_remote_copy(
            src_ref=src, dst_ref=dst, send_sem=ss, recv_sem=rs, device_id=dev, device_id_type=MESH
        )

    def zcopy(t, d, part):
        to = 4 * t - 2 + 2 * d
        fro = jnp.where(t == 1, 0, 4 * t - 6 + 2 * d)
        side, blocks = (1, A) if part == 2 else (0, (B, A)[part])
        return remote(
            col.at[fro + side, blocks], col.at[to + side, blocks], zs.at[d, t - 1, part], zr.at[d, t - 1, part], zdev[d]
        )

    def last_a():
        return remote(col.at[29, A], col.at[31, A], zs.at[1, 7, 2], zr.at[1, 7, 2], zdev[1])

    def last_b():
        return remote(col.at[29, B], col.at[31, B], zs.at[1, 7, 0], zr.at[1, 7, 0], zdev[1])

    def xown(part):
        blocks = (A, B)[part]
        return remote(col.at[0, blocks], col.at[1, blocks], xs.at[part, 0], xr.at[part, 0], xdev)

    def xcopy(t, d):
        slot = 4 * t - 2 + 2 * d
        return remote(col.at[slot, B], col.at[slot + 1, B], xs.at[d, t], xr.at[d, t], xdev)

    lanes_own = pl.ds(pl.multiple_of(256 * xl, 128), WIDE)
    lanes_far = pl.ds(pl.multiple_of(256 * (1 - xl), 128), WIDE)

    def pair(m):
        return pl.ds(2 * m, 2)

    def rows_copy(m, src, sems, dev):
        return remote(src, row.at[pair(m)], sems.at[m], rr.at[m], dev)

    def rows_wait(m):
        pltpu.make_async_copy(row.at[pair(m)], row.at[pair(m)], rr.at[m]).wait()

    def source_sends(m):
        src = col.at[pair(m), :, :, lanes_own]
        k = m % 2
        far = [
            remote(col.at[2 * m + s, :, :, lanes_far], row.at[2 * m + 1 - s], nears.at[m], rr.at[m], ndev(k))
            for s in (0, 1)
        ]
        return far, [
            rows_copy(m, src, ups, ydev(1, k)),
            rows_copy(m, src, downs, ydev(-1, k)),
            rows_copy(m, src, mates, mate),
        ]

    def source_start(m):
        far, rest = source_sends(m)
        for cp in far + rest:
            cp.start()
        pltpu.make_async_copy(col.at[pair(m), :, :, lanes_own], row.at[pair(m)], rr.at[m]).start()

    def relay_up(m):
        return is_near | ((dy == 1) & ((m // 2) % 2 == 0))

    def relay_down(m):
        return is_near | ((dy == 3) & ((m // 2) % 2 == 1))

    def relay(m):
        src = row.at[pair(m)]
        rows_wait(m)

        @pl.when(relay_up(m))
        def _():
            rows_copy(m, src, ups, ydev(1, core)).start()

        @pl.when(relay_down(m))
        def _():
            rows_copy(m, src, downs, ydev(-1, core)).start()

        rows_copy(m, src, mates, mate).start()

    def split(v):
        hi = v.astype(jnp.bfloat16)
        return hi, (v - hi.astype(jnp.float32)).astype(jnp.bfloat16)

    def compute(q, f):
        slots, blocks = pl.ds(8 * q, 8), pl.ds(4 * f, 4)
        w = row[slots, blocks].reshape(256, WIDE).T
        lhs[0], lhs[1] = split(w)
        v = col[slots, blocks].reshape(8, 2, 16, 640)
        for part, value in enumerate(split(v)):
            rhs[part, :, :640] = value.reshape(256, 640)
            swapped = jnp.concatenate([-value[:, 1:2], value[:, 0:1]], axis=1)
            rhs[part, :, 640:] = swapped.reshape(256, 640)
        rows = pl.ds(pl.multiple_of(64 * xl, 64), 320)
        l_hi, l_lo = lhs[0, rows], lhs[1, rows]
        for n in range(5):
            lanes = slice(256 * n, 256 * n + 256)
            r_hi, r_lo = rhs[0, :, lanes], rhs[1, :, lanes]
            total = jnp.dot(l_hi, r_hi, preferred_element_type=jnp.float32)
            total += jnp.dot(l_lo, r_hi, preferred_element_type=jnp.float32)
            total += jnp.dot(l_hi, r_lo, preferred_element_type=jnp.float32)
            for half in (0, 1):
                at = 256 * n + 128 * half
                p, j = at // 640, at % 640
                out_ref[f, p, :, j : j + 128] += total[:, 128 * half : 128 * half + 128]

    for d in (0, 1):
        zcopy(1, d, 0).start()
        zcopy(1, d, 1).start()
    xown(0).start()
    xown(1).start()
    out_ref[...] = jnp.zeros_like(out_ref)
    xown(0).wait_recv()
    for d in (0, 1):
        zcopy(1, d, 2).start()

    def step(k, carry):
        @pl.when(k <= 7)
        def _():
            for part in (0, 1, 2):
                for d in (0, 1):
                    zcopy(k, d, part).wait_recv()

                    @pl.when(k < 7)
                    def _():
                        zcopy(k + 1, d, part).start()

                    if part == 0:
                        xcopy(k, d).start()
                    if part < 2 and d == 0:

                        @pl.when(k == 7)
                        def _():
                            zcopy(k + 1, d, part).start()

                    if part == 2 and d == 1:

                        @pl.when(k == 7)
                        def _():
                            last_a().start()

        @pl.when(k == 1)
        def _():
            xown(1).wait_recv()

        @pl.when((k >= 2) & (k <= 8))
        def _():
            for d in (0, 1):
                xcopy(k - 1, d).wait_recv()

        @pl.when(k == 8)
        def _():
            last_b().start()
            zcopy(k, 0, 0).wait_recv()
            zcopy(k, 0, 1).wait_recv()
            last_a().wait_recv()

        @pl.when(k == 9)
        def _():
            last_b().wait_recv()

        for m in (2 * k - 3, 2 * k - 2):

            @pl.when(is_src & (m >= 0) & (m <= 15))
            def _():
                source_start(m)

        m = 2 * (k - lag) - core

        @pl.when(plain & (m >= 0) & (m <= 15))
        def _():
            relay(m)

        at = k - lag - 3
        q, f = at // 2, at % 2

        @pl.when((at >= 0) & (at <= 7))
        def _():
            @pl.when(f == 0)
            def _():
                for i in range(4):

                    @pl.when(jnp.logical_not(plain) | (i % 2 != core))
                    def _():
                        rows_wait(4 * q + i)

            compute(q, f)

        return carry

    lax.fori_loop(1, 16, step, 0)

    def zdone(t, carry):
        for d in (0, 1):
            for part in (0, 1, 2):
                zcopy(t, d, part).wait_send()
            xcopy(t, d).wait_send()
        return carry

    lax.fori_loop(1, 8, zdone, 0)
    zcopy(8, 0, 0).wait_send()
    zcopy(8, 0, 1).wait_send()
    last_a().wait_send()
    last_b().wait_send()
    xown(0).wait_send()
    xown(1).wait_send()

    def rdone(m, carry):
        mine = plain & (m % 2 == core)
        src = row.at[pair(m)]

        @pl.when(is_src)
        def _():
            rows_copy(m, src, nears, mate).wait_send()

        @pl.when(is_src | (mine & relay_up(m)))
        def _():
            rows_copy(m, src, ups, mate).wait_send()

        @pl.when(is_src | (mine & relay_down(m)))
        def _():
            rows_copy(m, src, downs, mate).wait_send()

        @pl.when(is_src | mine)
        def _():
            rows_copy(m, src, mates, mate).wait_send()

        return carry

    lax.fori_loop(0, 16, rdone, 0)


def per_device(spectra):
    shard = spectra.reshape(8, 8, 640)
    dma = pltpu.SemaphoreType.DMA
    sums = pl.pallas_call(
        kernel,
        out_shape=jax.ShapeDtypeStruct((2, 2, 320, 640), jnp.float32),
        in_specs=[pl.BlockSpec(memory_space=pl.ANY)],
        out_specs=pl.BlockSpec(memory_space=pltpu.VMEM),
        scratch_shapes=[
            pltpu.VMEM((32, 8, 8, 640), jnp.float32),
            pltpu.VMEM((32, 8, 8, WIDE), jnp.float32),
            pltpu.VMEM((2, WIDE, 256), jnp.bfloat16),
            pltpu.VMEM((2, 256, 1280), jnp.bfloat16),
            dma,
            dma((2, 8, 3)),
            dma((2, 8, 3)),
            dma((2, 8)),
            dma((2, 8)),
            dma((16,)),
            dma((16,)),
            dma((16,)),
            dma((16,)),
            dma((16,)),
        ],
        compiler_params=pltpu.CompilerParams(
            collective_id=0, has_side_effects=True, vmem_limit_bytes=28 * 2**20
        ),
        name="gather_and_multiply",
    )(shard)
    return sums * (1.0 / 512.0)


def solution(mesh):
    return jax.shard_map(
        per_device,
        mesh=mesh,
        in_specs=(P(None, None, "row", "col"),),
        out_specs=P(None, None, "row", "col"),
        check_vma=False,
    )
```

time: 349 us -> 81.4 us (0.23)
  the two profiles are of different devices: /device:TPU:1 before, /device:TPU:20 now
where the time goes in v1:
time: 81.4 us; the launch traced here: 81.2 us
  Pallas kernels  78.4 us (96%)
  other arithmetic  1.92 us (2%)
  local copies, waits for them, and re-layouts  0.92 us (1%)
    pallas_call x1, Pallas kernels, per_device(): pl.pallas_call(kernel, out_shape=jax.ShapeDtypeStruct((2, 2, 320, 640), j...  78.4 us
    mul x1, other arithmetic, per_device(): return sums * (1.0 / 512.0)  1.92 us

profile of v1, /device:TPU:20, one launch (start us, length us, event | category | flops | bytes accessed | tf_op | source)
XLA Modules:
  0.0 81.2 jit_solution(7357479500498094969)
XLA Ops:
  0.0 0.0 copy-start
  0.0 0.9 %copy-done = f32[2,2,16,640]{3,2,1,0:T(8,128)S(1)} copy-done((f32[2,2,16,640]{3,2,1,0:T(8,128)S(1)}, f32[2,2,16,640]{3,2,1,0:T(8,128)}, u32[]{:S(2)}) %copy-start) | copy-done | bytes 163864
  0.9 78.4 %gather_and_multiply.1 = f32[2,2,320,640]{3,2,1,0:T(8,128)S(1)} custom-call(f32[8,8,640]{2,1,0:T(8,128)S(1)} %bitcast.1), custom_call_target="tpu_custom_call" | custom-call | tf_op jit(solution)/shard_map/gather_and_multiply/pallas_call | solution.py:283
  79.3 1.9 %broadcast_multiply_fusion = f32[2,2,320,640]{3,2,1,0:T(8,128)} fusion(f32[2,2,320,640]{3,2,1,0:T(8,128)S(1)} %gather_and_multiply.1), kind=kLoop, calls=%fused_computation | loop fusion | flops 819200 | bytes 6553600 | tf_op jit(solution)/shard_map/mul | solution.py:309
Async XLA Ops:
  0.0 0.9 %copy-start = (f32[2,2,16,640]{3,2,1,0:T(8,128)S(1)}, f32[2,2,16,640]{3,2,1,0:T(8,128)}, u32[]{:S(2)}) copy-start(f32[2,2,16,640]{3,2,1,0:T(8,128)} %param.1) | copy-start | bytes 491524

commit v2 on v1

v2 whole, which is shorter than its diff:
```python
import jax
import jax.numpy as jnp
from jax import lax
from jax.experimental import pallas as pl
from jax.experimental.pallas import tpu as pltpu
from jax.sharding import PartitionSpec as P

MESH = pl.DeviceIdType.MESH
CUT = 3
HALF = 10
TILES = 2 * HALF


def kernel(x_ref, out_ref, col, row, far, lhs, rhs, own_sem, zs, zr, xs, xr, rr, ups, downs, mates, nears):
    r = lax.axis_index("row")
    c = lax.axis_index("col")
    z, xl = r // 2, r % 2
    xh, y, core = c // 8, (c // 2) % 4, c % 2
    src_xh, src_y, src_core = z // 8, (z // 2) % 4, z % 2
    dy = (y - src_y + 4) % 4
    home = xh == src_xh
    is_src = home & (dy == 0) & (core == src_core)
    is_src_mate = home & (dy == 0) & (core != src_core)
    is_near = jnp.logical_not(home) & (dy == 0)
    plain = jnp.logical_not(is_src | is_src_mate)
    hops = jnp.where(home, 0, 1) + jnp.where(dy == 0, 0, 1) + jnp.where(dy == 2, 1, 0)
    lag = jnp.maximum(hops - 1, 0)
    turns = (hops + 1 + jnp.where(hops == 3, 1, 0), 2 * hops + jnp.where(hops == 3, 0, 1))
    flip = jnp.where(home, 0, 1)

    zdev = [((r + 2) % 32, c), ((r + 30) % 32, c)]
    xdev = (r + 1 - 2 * xl, c)
    mate = (r, c + 1 - 2 * core)

    def ydev(step, k):
        return (r, xh * 8 + ((y + step + 4) % 4) * 2 + k)

    def ndev(k):
        return (r + 1 - 2 * xl, (1 - xh) * 8 + y * 2 + k)

    own = pltpu.make_async_copy(x_ref, col.at[0], own_sem)
    own.start()
    barrier = pltpu.get_barrier_semaphore()
    greet = [zdev[0], zdev[1], xdev, mate]
    greet += [ydev(s, k) for s in (1, -1) for k in (0, 1)] + [ndev(0), ndev(1)]
    for d in greet:
        pl.semaphore_signal(barrier, inc=1, device_id=d, device_id_type=MESH)
    own.wait()
    pl.semaphore_wait(barrier, len(greet))

    A, B = pl.ds(0, CUT), pl.ds(CUT, 8 - CUT)

    def remote(src, dst, ss, rs, dev):
        return pltpu.make_async_remote_copy(
            src_ref=src, dst_ref=dst, send_sem=ss, recv_sem=rs, device_id=dev, device_id_type=MESH
        )

    def zcopy(t, d, part):
        to = 4 * t - 2 + 2 * d
        fro = jnp.where(t == 1, 0, 4 * t - 6 + 2 * d)
        side, blocks = (1, A) if part == 2 else (0, (B, A)[part])
        return remote(
            col.at[fro + side, blocks], col.at[to + side, blocks], zs.at[d, t - 1, part], zr.at[d, t - 1, part], zdev[d]
        )

    def last_a():
        return remote(col.at[29, A], col.at[31, A], zs.at[1, 7, 2], zr.at[1, 7, 2], zdev[1])

    def last_b():
        return remote(col.at[29, B], col.at[31, B], zs.at[1, 7, 0], zr.at[1, 7, 0], zdev[1])

    def xown(part):
        blocks = (A, B)[part]
        return remote(col.at[0, blocks], col.at[1, blocks], xs.at[part, 0], xr.at[part, 0], xdev)

    def xcopy(t, d):
        slot = 4 * t - 2 + 2 * d
        return remote(col.at[slot, B], col.at[slot + 1, B], xs.at[d, t], xr.at[d, t], xdev)

    def half(f):
        return pl.ds(HALF * f, HALF)

    def rows_copy(s, f, src, sems, dev, to=None):
        to = s if to is None else to
        return remote(src.at[s, half(f)], row.at[to, half(f)], sems.at[s], rr.at[2 * to + f], dev)

    def rows_wait(s, f):
        pltpu.make_async_copy(row.at[s, half(f)], row.at[s, half(f)], rr.at[2 * s + f]).wait()

    def sent(s, sems):
        remote(row.at[s], row.at[s], sems.at[s], rr.at[2 * s], mate).wait_send()

    def other(s):
        return s + 1 - 2 * (s % 2)

    def pack(s):
        low = lax.broadcasted_iota(jnp.int32, (32, 128), 1) < 64
        mid = col[s, :, :, 256:384].reshape(2, 2, 2, 8, 128)
        re, im = mid[:, 0].reshape(32, 128), mid[:, 1].reshape(32, 128)
        first = jnp.where(low, re, pltpu.roll(im, 64, 1))
        second = jnp.where(low, pltpu.roll(re, 64, 1), im)
        for buf, side in ((row, xl), (far, 1 - xl)):
            packed = jnp.where(side == 0, first, second).reshape(2, 2, 8, 128)
            for f in (0, 1):
                for a in (0, 1):
                    lanes = pl.ds(pl.multiple_of(384 * side + 128 * a, 128), 128)
                    at = HALF * f + 4 * a
                    buf[s, at : at + 4] = col[s, 4 * f : 4 * f + 4, :, lanes]
                buf[s, HALF * f + 8 : HALF * f + 10] = packed[f]

    def source_start(s):
        pack(s)
        k = (s // 2) % 2
        for f in (0, 1):
            rows_copy(s, f, far, nears, ndev(k), other(s)).start()
            rows_copy(s, f, row, ups, ydev(1, k)).start()
            rows_copy(s, f, row, downs, ydev(-1, k)).start()
            rows_copy(s, f, row, mates, mate).start()

    def relay_up(kind):
        return is_near | ((dy == 1) & (kind == 0))

    def relay_down(kind):
        return is_near | ((dy == 3) & (kind == 1))

    def relay(s, kind):
        for f in (0, 1):
            rows_wait(s, f)

            @pl.when(relay_up(kind))
            def _():
                rows_copy(s, f, row, ups, ydev(1, core)).start()

            @pl.when(relay_down(kind))
            def _():
                rows_copy(s, f, row, downs, ydev(-1, core)).start()

            rows_copy(s, f, row, mates, mate).start()

    def split(v):
        hi = v.astype(jnp.bfloat16)
        return hi, (v - hi.astype(jnp.float32)).astype(jnp.bfloat16)

    def compute(q, f):
        slots = pl.ds(8 * q, 8)
        for p in (0, 1):
            depth = slice(128 * p, 128 * p + 128)
            for a in (0, 1):
                w = row[slots, pl.ds(HALF * f + 4 * a + 2 * p, 2)].reshape(128, 128).T
                at = pl.ds(pl.multiple_of(64 * xl + 128 * a, 64), 128)
                lhs[0, at, depth], lhs[1, at, depth] = split(w)
        w = row[slots, pl.ds(HALF * f + 8, 2)].reshape(128, 128).T
        at = pl.ds(pl.multiple_of(256 * (1 - xl), 64), 64)
        for part, value in enumerate(split(w)):
            lhs[part, at, :128], lhs[part, at, 128:] = value[:64], value[64:]
        for part, (re, im) in enumerate(zip(*[split(col[slots, pl.ds(4 * f + 2 * p, 2)].reshape(128, 640)) for p in (0, 1)])):
            rhs[part, :128, :640], rhs[part, 128:, :640] = re, im
            rhs[part, :128, 640:], rhs[part, 128:, 640:] = -im, re
        l_hi, l_lo = lhs[0], lhs[1]
        for n in range(5):
            lanes = slice(256 * n, 256 * n + 256)
            r_hi, r_lo = rhs[0, :, lanes], rhs[1, :, lanes]
            total = jnp.dot(l_hi, r_hi, preferred_element_type=jnp.float32)
            total += jnp.dot(l_lo, r_hi, preferred_element_type=jnp.float32)
            total += jnp.dot(l_hi, r_lo, preferred_element_type=jnp.float32)
            for half in (0, 1):
                at = 256 * n + 128 * half
                p, j = at // 640, at % 640
                out_ref[f, p, :, j : j + 128] += total[:, 128 * half : 128 * half + 128]

    for d in (0, 1):
        zcopy(1, d, 0).start()
        zcopy(1, d, 1).start()
    xown(0).start()
    xown(1).start()
    out_ref[...] = jnp.zeros_like(out_ref)
    xown(0).wait_recv()
    for d in (0, 1):
        zcopy(1, d, 2).start()

    def source_sends(at, kind):
        for d in (0, 1):
            s = 4 * at - 2 + 2 * d + kind

            @pl.when(is_src & (s >= 0) & (s <= 31))
            def _():
                source_start(s)

    def step(k, carry):
        ring = (k >= 1) & (k <= 7)

        def arrive(part):
            for d in (1, 0):
                zcopy(k, d, part).wait_recv()

                @pl.when(k < 7)
                def _():
                    zcopy(k + 1, d, part).start()

                if part == 0:
                    xcopy(k, d).start()
                if part < 2 and d == 0:

                    @pl.when(k == 7)
                    def _():
                        zcopy(k + 1, d, part).start()

                if part == 2 and d == 1:

                    @pl.when(k == 7)
                    def _():
                        last_a().start()

        def relays(turn):
            for kind in (1, 0):
                t = turn - turns[kind]
                s = 2 * t - 2 * core + (flip if kind == 0 else 1 - flip)

                @pl.when(plain & (t % 2 == 0) & (s >= 0) & (s <= 31))
                def _():
                    relay(s, kind)

        @pl.when(ring)
        def _():
            arrive(0)

        @pl.when(k == 1)
        def _():
            xown(1).wait_recv()

        @pl.when((k >= 2) & (k <= 8))
        def _():
            xcopy(k - 1, 1).wait_recv()

            @pl.when(k == 8)
            def _():
                last_b().start()

            xcopy(k - 1, 0).wait_recv()

        @pl.when(k == 9)
        def _():
            last_a().wait_recv()
            last_b().wait_recv()

        source_sends(k - 1, 1)
        relays(2 * k)

        @pl.when(ring)
        def _():
            arrive(1)

        @pl.when(k == 8)
        def _():
            zcopy(k, 0, 0).wait_recv()
            zcopy(k, 0, 1).wait_recv()

        source_sends(k, 0)

        at = k - lag - 4
        q, f = at // 2, at % 2

        @pl.when((at >= 0) & (at <= 7))
        def _():
            for i in range(8):

                @pl.when(is_src_mate | (plain & ((i // 2) % 2 != core)))
                def _():
                    rows_wait(8 * q + i, f)

            compute(q, f)

        @pl.when(ring)
        def _():
            arrive(2)

        relays(2 * k + 1)
        return carry

    lax.fori_loop(0, 14, step, 0)

    def zdone(t, carry):
        for d in (0, 1):
            for part in (0, 1, 2):
                zcopy(t, d, part).wait_send()
            xcopy(t, d).wait_send()
        return carry

    lax.fori_loop(1, 8, zdone, 0)
    zcopy(8, 0, 0).wait_send()
    zcopy(8, 0, 1).wait_send()
    last_a().wait_send()
    last_b().wait_send()
    xown(0).wait_send()
    xown(1).wait_send()

    def rdone(s, carry):
        mine = plain & ((s // 2) % 2 == core)
        kind = (s + flip) % 2

        @pl.when(is_src)
        def _():
            sent(s, nears)

        @pl.when(is_src | (mine & relay_up(kind)))
        def _():
            sent(s, ups)

        @pl.when(is_src | (mine & relay_down(kind)))
        def _():
            sent(s, downs)

        @pl.when(is_src | mine)
        def _():
            sent(s, mates)

        return carry

    lax.fori_loop(0, 32, rdone, 0)


def per_device(spectra):
    shard = spectra.reshape(8, 8, 640)
    dma = pltpu.SemaphoreType.DMA
    sums = pl.pallas_call(
        kernel,
        out_shape=jax.ShapeDtypeStruct((2, 2, 320, 640), jnp.float32),
        in_specs=[pl.BlockSpec(memory_space=pltpu.HBM)],
        out_specs=pl.BlockSpec(memory_space=pltpu.VMEM),
        scratch_shapes=[
            pltpu.VMEM((32, 8, 8, 640), jnp.float32),
            pltpu.VMEM((32, TILES, 8, 128), jnp.float32),
            pltpu.VMEM((32, TILES, 8, 128), jnp.float32),
            pltpu.VMEM((2, 320, 256), jnp.bfloat16),
            pltpu.VMEM((2, 256, 1280), jnp.bfloat16),
            dma,
            dma((2, 8, 3)),
            dma((2, 8, 3)),
            dma((2, 8)),
            dma((2, 8)),
            dma((64,)),
            dma((32,)),
            dma((32,)),
            dma((32,)),
            dma((32,)),
        ],
        compiler_params=pltpu.CompilerParams(
            collective_id=0, has_side_effects=True, vmem_limit_bytes=28 * 2**20
        ),
        name="gather_and_multiply",
    )(pltpu.with_memory_space_constraint(shard, pltpu.HBM))
    return sums * (1.0 / 512.0)


def solution(mesh):
    return jax.shard_map(
        per_device,
        mesh=mesh,
        in_specs=(P(None, None, "row", "col"),),
        out_specs=P(None, None, "row", "col"),
        check_vma=False,
    )
```

time: 81.4 us -> 71.9 us (0.88)
  the two profiles are of different devices: /device:TPU:20 before, /device:TPU:23 now
where the time goes in v2:
time: 71.9 us; the launch traced here: 71.3 us
  Pallas kernels  69.4 us (97%)
  other arithmetic  1.92 us (3%)
    pallas_call x1, Pallas kernels, per_device(): pl.pallas_call(kernel, out_shape=jax.ShapeDtypeStruct((2, 2, 320, 640), j...  69.4 us
    mul x1, other arithmetic, per_device(): return sums * (1.0 / 512.0)  1.92 us

profile of v2, /device:TPU:23, one launch (start us, length us, event | category | flops | bytes accessed | tf_op | source)
XLA Modules:
  0.0 71.3 jit_solution(17464461117800206078)
XLA Ops:
  0.0 69.4 %gather_and_multiply.1 = f32[2,2,320,640]{3,2,1,0:T(8,128)S(1)} custom-call(f32[8,8,640]{2,1,0:T(8,128)} %bitcast.1), custom_call_target="tpu_custom_call" | custom-call | tf_op jit(solution)/shard_map/gather_and_multiply/pallas_call | solution.py:325
  69.4 1.9 %broadcast_multiply_fusion = f32[2,2,320,640]{3,2,1,0:T(8,128)} fusion(f32[2,2,320,640]{3,2,1,0:T(8,128)S(1)} %gather_and_multiply.1), kind=kLoop, calls=%fused_computation | loop fusion | flops 819200 | bytes 6553600 | tf_op jit(solution)/shard_map/mul | solution.py:352

commit v3 on v2

--- a/solution.py
+++ b/solution.py
@@ -8,10 +8,12 @@
 MESH = pl.DeviceIdType.MESH
 CUT = 3
 HALF = 10
+PAD = 2
 TILES = 2 * HALF
 
 
-def kernel(x_ref, out_ref, col, row, far, lhs, rhs, own_sem, zs, zr, xs, xr, rr, ups, downs, mates, nears):
+def kernel(x_ref, out_ref, col, row, far, lhs, rhs, own_sem, zs, zr, xs, xr, rr, rs):
+    ups, downs, mates, nears = 0, 1, 2, 3
     r = lax.axis_index("row")
     c = lax.axis_index("col")
     z, xl = r // 2, r % 2
@@ -24,7 +26,7 @@
     is_near = jnp.logical_not(home) & (dy == 0)
     plain = jnp.logical_not(is_src | is_src_mate)
     hops = jnp.where(home, 0, 1) + jnp.where(dy == 0, 0, 1) + jnp.where(dy == 2, 1, 0)
-    lag = jnp.maximum(hops - 1, 0)
+    lag = jnp.where(hops >= 2, 1, 0)
     turns = (hops + 1 + jnp.where(hops == 3, 1, 0), 2 * hops + jnp.where(hops == 3, 0, 1))
     flip = jnp.where(home, 0, 1)
 
@@ -38,7 +40,10 @@
     def ndev(k):
         return (r + 1 - 2 * xl, (1 - xh) * 8 + y * 2 + k)
 
-    own = pltpu.make_async_copy(x_ref, col.at[0], own_sem)
+    def blk(s, blocks):
+        return pl.ds(8 * (s + PAD) + blocks.start, blocks.stop - blocks.start)
+
+    own = pltpu.make_async_copy(x_ref, col.at[blk(0, slice(0, 8))], own_sem)
     own.start()
     barrier = pltpu.get_barrier_semaphore()
     greet = [zdev[0], zdev[1], xdev, mate]
@@ -48,7 +53,7 @@
     own.wait()
     pl.semaphore_wait(barrier, len(greet))
 
-    A, B = pl.ds(0, CUT), pl.ds(CUT, 8 - CUT)
+    A, B = slice(0, CUT), slice(CUT, 8)
 
     def remote(src, dst, ss, rs, dev):
         return pltpu.make_async_remote_copy(
@@ -60,42 +65,45 @@
         fro = jnp.where(t == 1, 0, 4 * t - 6 + 2 * d)
         side, blocks = (1, A) if part == 2 else (0, (B, A)[part])
         return remote(
-            col.at[fro + side, blocks], col.at[to + side, blocks], zs.at[d, t - 1, part], zr.at[d, t - 1, part], zdev[d]
+            col.at[blk(fro + side, blocks)], col.at[blk(to + side, blocks)], zs.at[d], zr.at[d, t - 1, part], zdev[d]
         )
 
     def last_a():
-        return remote(col.at[29, A], col.at[31, A], zs.at[1, 7, 2], zr.at[1, 7, 2], zdev[1])
+        return remote(col.at[blk(29, A)], col.at[blk(31, A)], zs.at[1], zr.at[1, 7, 2], zdev[1])
 
     def last_b():
-        return remote(col.at[29, B], col.at[31, B], zs.at[1, 7, 0], zr.at[1, 7, 0], zdev[1])
+        return remote(col.at[blk(29, B)], col.at[blk(31, B)], zs.at[1], zr.at[1, 7, 0], zdev[1])
 
     def xown(part):
         blocks = (A, B)[part]
-        return remote(col.at[0, blocks], col.at[1, blocks], xs.at[part, 0], xr.at[part, 0], xdev)
+        return remote(col.at[blk(0, blocks)], col.at[blk(1, blocks)], xs, xr.at[part, 0], xdev)
 
     def xcopy(t, d):
         slot = 4 * t - 2 + 2 * d
-        return remote(col.at[slot, B], col.at[slot + 1, B], xs.at[d, t], xr.at[d, t], xdev)
+        return remote(col.at[blk(slot, B)], col.at[blk(slot + 1, B)], xs, xr.at[d, t], xdev)
 
     def half(f):
         return pl.ds(HALF * f, HALF)
 
-    def rows_copy(s, f, src, sems, dev, to=None):
+    def rows_copy(s, f, src, way, dev, to=None):
         to = s if to is None else to
-        return remote(src.at[s, half(f)], row.at[to, half(f)], sems.at[s], rr.at[2 * to + f], dev)
+        return remote(src.at[s + PAD, half(f)], row.at[to + PAD, half(f)], rs.at[way], rr.at[2 * to + f], dev)
 
     def rows_wait(s, f):
-        pltpu.make_async_copy(row.at[s, half(f)], row.at[s, half(f)], rr.at[2 * s + f]).wait()
-
-    def sent(s, sems):
-        remote(row.at[s], row.at[s], sems.at[s], rr.at[2 * s], mate).wait_send()
+        ref = row.at[s + PAD, half(f)]
+        pltpu.make_async_copy(ref, ref, rr.at[2 * s + f]).wait()
+
+    def sent(shards, way):
+        ref = row.at[pl.ds(0, shards)]
+        remote(ref, ref, rs.at[way], rr.at[0], mate).wait_send()
 
     def other(s):
         return s + 1 - 2 * (s % 2)
 
     def pack(s):
         low = lax.broadcasted_iota(jnp.int32, (32, 128), 1) < 64
-        mid = col[s, :, :, 256:384].reshape(2, 2, 2, 8, 128)
+        shard = pl.ds(8 * (s + PAD), 8)
+        mid = col[shard, :, 256:384].reshape(2, 2, 2, 8, 128)
         re, im = mid[:, 0].reshape(32, 128), mid[:, 1].reshape(32, 128)
         first = jnp.where(low, re, pltpu.roll(im, 64, 1))
         second = jnp.where(low, pltpu.roll(re, 64, 1), im)
@@ -105,8 +113,8 @@
                 for a in (0, 1):
                     lanes = pl.ds(pl.multiple_of(384 * side + 128 * a, 128), 128)
                     at = HALF * f + 4 * a
-                    buf[s, at : at + 4] = col[s, 4 * f : 4 * f + 4, :, lanes]
-                buf[s, HALF * f + 8 : HALF * f + 10] = packed[f]
+                    buf[s + PAD, at : at + 4] = col[pl.ds(8 * (s + PAD) + 4 * f, 4), :, lanes]
+                buf[s + PAD, HALF * f + 8 : HALF * f + 10] = packed[f]
 
     def source_start(s):
         pack(s)
@@ -140,6 +148,17 @@
     def split(v):
         hi = v.astype(jnp.bfloat16)
         return hi, (v - hi.astype(jnp.float32)).astype(jnp.bfloat16)
+
+    def add(f, n, total):
+        for side in (0, 1):
+            at = 256 * n + 128 * side
+            p, j = at // 640, at % 640
+            out_ref[f, p, :, j : j + 128] += total[:, 128 * side : 128 * side + 128]
+
+    def rhs_store(part, at, re, im):
+        n = re.shape[0]
+        rhs[part, at : at + n, :640], rhs[part, at + n : at + 2 * n, :640] = re, im
+        rhs[part, at : at + n, 640:], rhs[part, at + n : at + 2 * n, 640:] = -im, re
 
     def compute(q, f):
         slots = pl.ds(8 * q, 8)
@@ -153,9 +172,12 @@
         at = pl.ds(pl.multiple_of(256 * (1 - xl), 64), 64)
         for part, value in enumerate(split(w)):
             lhs[part, at, :128], lhs[part, at, 128:] = value[:64], value[64:]
-        for part, (re, im) in enumerate(zip(*[split(col[slots, pl.ds(4 * f + 2 * p, 2)].reshape(128, 640)) for p in (0, 1)])):
-            rhs[part, :128, :640], rhs[part, 128:, :640] = re, im
-            rhs[part, :128, 640:], rhs[part, 128:, 640:] = -im, re
+        col4 = col.reshape(32 + PAD, 8, 8, 640)
+        (re_hi, re_lo), (im_hi, im_lo) = [
+            split(col4[slots, pl.ds(4 * f + 2 * p, 2)].reshape(128, 640)) for p in (0, 1)
+        ]
+        rhs_store(0, 0, re_hi, im_hi)
+        rhs_store(1, 0, re_lo, im_lo)
         l_hi, l_lo = lhs[0], lhs[1]
         for n in range(5):
             lanes = slice(256 * n, 256 * n + 256)
@@ -163,10 +185,32 @@
             total = jnp.dot(l_hi, r_hi, preferred_element_type=jnp.float32)
             total += jnp.dot(l_lo, r_hi, preferred_element_type=jnp.float32)
             total += jnp.dot(l_hi, r_lo, preferred_element_type=jnp.float32)
-            for half in (0, 1):
-                at = 256 * n + 128 * half
-                p, j = at // 640, at % 640
-                out_ref[f, p, :, j : j + 128] += total[:, 128 * half : 128 * half + 128]
+            add(f, n, total)
+
+    def compute_last(f):
+        slots = slice(30 + PAD, 32 + PAD)
+
+        def stacked(w):
+            hi = w.astype(jnp.bfloat16).astype(jnp.float32)
+            return jnp.concatenate([hi, w - hi, hi, jnp.zeros_like(w)], axis=0).T.astype(jnp.bfloat16)
+
+        for a in (0, 1):
+            w = [row[slots, HALF * f + 4 * a + 2 * p : HALF * f + 4 * a + 2 * p + 2].reshape(32, 128) for p in (0, 1)]
+            lhs[0, pl.ds(pl.multiple_of(64 * xl + 128 * a, 64), 128)] = stacked(jnp.concatenate(w, axis=0))
+        w = row[slots, HALF * f + 8 : HALF * f + 10].reshape(32, 128)
+        w = stacked(jnp.concatenate([w, pltpu.roll(w, 64, 1)], axis=0))
+        lhs[0, pl.ds(pl.multiple_of(256 * (1 - xl), 64), 64)] = w[:64]
+        col4 = col.reshape(32 + PAD, 8, 8, 640)
+        (re_hi, re_lo), (im_hi, im_lo) = [
+            split(col4[slots, 4 * f + 2 * p : 4 * f + 2 * p + 2].reshape(32, 640)) for p in (0, 1)
+        ]
+        rhs_store(0, 0, re_hi, im_hi)
+        rhs_store(0, 64, re_hi, im_hi)
+        rhs_store(0, 128, re_lo, im_lo)
+        rhs[0, 192:] = jnp.zeros((64, 1280), jnp.bfloat16)
+        left = lhs[0]
+        for n in range(5):
+            add(f, n, jnp.dot(left, rhs[0, :, 256 * n : 256 * n + 256], preferred_element_type=jnp.float32))
 
     for d in (0, 1):
         zcopy(1, d, 0).start()
@@ -174,6 +218,8 @@
     xown(0).start()
     xown(1).start()
     out_ref[...] = jnp.zeros_like(out_ref)
+    col[: 8 * PAD] = jnp.zeros((8 * PAD, 8, 640), jnp.float32)
+    row[:PAD] = jnp.zeros((PAD, TILES, 8, 128), jnp.float32)
     xown(0).wait_recv()
     for d in (0, 1):
         zcopy(1, d, 2).start()
@@ -185,6 +231,17 @@
             @pl.when(is_src & (s >= 0) & (s <= 31))
             def _():
                 source_start(s)
+
+    def others_wait(s, f):
+        @pl.when((s >= 0) & (is_src_mate | (plain & ((s // 2) % 2 != core))))
+        def _():
+            rows_wait(s, f)
+
+    def waited(at):
+        q, f = at // 2, at % 2
+        for i in range(8):
+            others_wait(8 * q + i - PAD, f)
+        compute(q, f)
 
     def step(k, carry):
         ring = (k >= 1) & (k <= 7)
@@ -257,66 +314,60 @@
 
         source_sends(k, 0)
 
-        at = k - lag - 4
-        q, f = at // 2, at % 2
-
-        @pl.when((at >= 0) & (at <= 7))
-        def _():
-            for i in range(8):
-
-                @pl.when(is_src_mate | (plain & ((i // 2) % 2 != core)))
-                def _():
-                    rows_wait(8 * q + i, f)
-
-            compute(q, f)
+        at = k - 3 - lag
+
+        @pl.when((k <= 7) & (at >= 0))
+        def _():
+            waited(at)
 
         @pl.when(ring)
         def _():
             arrive(2)
 
         relays(2 * k + 1)
+        at = jnp.where(hops == 3, k - 4, k - jnp.where(k <= 8, 2, 3) - lag)
+        early = (k >= 7) & (k <= 8) & (at <= 5)
+        late = (k >= 9) & (at >= jnp.where(hops == 3, 5, 6)) & (at <= 7)
+
+        @pl.when(jnp.where(hops == 3, k >= 8, early | late))
+        def _():
+            waited(at)
+
         return carry
 
-    lax.fori_loop(0, 14, step, 0)
-
-    def zdone(t, carry):
-        for d in (0, 1):
-            for part in (0, 1, 2):
-                zcopy(t, d, part).wait_send()
-            xcopy(t, d).wait_send()
-        return carry
-
-    lax.fori_loop(1, 8, zdone, 0)
-    zcopy(8, 0, 0).wait_send()
-    zcopy(8, 0, 1).wait_send()
-    last_a().wait_send()
-    last_b().wait_send()
-    xown(0).wait_send()
-    xown(1).wait_send()
-
-    def rdone(s, carry):
-        mine = plain & ((s // 2) % 2 == core)
-        kind = (s + flip) % 2
-
-        @pl.when(is_src)
-        def _():
-            sent(s, nears)
-
-        @pl.when(is_src | (mine & relay_up(kind)))
-        def _():
-            sent(s, ups)
-
-        @pl.when(is_src | (mine & relay_down(kind)))
-        def _():
-            sent(s, downs)
-
-        @pl.when(is_src | mine)
-        def _():
-            sent(s, mates)
-
-        return carry
-
-    lax.fori_loop(0, 32, rdone, 0)
+    lax.fori_loop(0, 12, step, 0)
+    for f in (0, 1):
+        for s in (30, 31):
+            others_wait(s, f)
+        compute_last(f)
+
+    for d in (0, 1):
+        ref = col.at[pl.ds(0, 7 * (8 + CUT) + 8)]
+        remote(ref, ref, zs.at[d], zr.at[0, 0, 0], mate).wait_send()
+    ref = col.at[pl.ds(0, 8 + 14 * (8 - CUT))]
+    remote(ref, ref, xs, zr.at[0, 0, 0], mate).wait_send()
+
+    @pl.when(is_src)
+    def _():
+        for way in (ups, downs, mates, nears):
+            sent(32, way)
+
+    @pl.when(is_near)
+    def _():
+        sent(16, ups)
+        sent(16, downs)
+
+    @pl.when(dy == 1)
+    def _():
+        sent(8, ups)
+
+    @pl.when(dy == 3)
+    def _():
+        sent(8, downs)
+
+    @pl.when(plain)
+    def _():
+        sent(16, mates)
 
 
 def per_device(spectra):
@@ -328,21 +379,18 @@
         in_specs=[pl.BlockSpec(memory_space=pltpu.HBM)],
         out_specs=pl.BlockSpec(memory_space=pltpu.VMEM),
         scratch_shapes=[
-            pltpu.VMEM((32, 8, 8, 640), jnp.float32),
-            pltpu.VMEM((32, TILES, 8, 128), jnp.float32),
-            pltpu.VMEM((32, TILES, 8, 128), jnp.float32),
+            pltpu.VMEM((8 * (32 + PAD), 8, 640), jnp.float32),
+            pltpu.VMEM((32 + PAD, TILES, 8, 128), jnp.float32),
+            pltpu.VMEM((32 + PAD, TILES, 8, 128), jnp.float32),
             pltpu.VMEM((2, 320, 256), jnp.bfloat16),
             pltpu.VMEM((2, 256, 1280), jnp.bfloat16),
             dma,
+            dma((2,)),
             dma((2, 8, 3)),
-            dma((2, 8, 3)),
-            dma((2, 8)),
+            dma,
             dma((2, 8)),
             dma((64,)),
-            dma((32,)),
-            dma((32,)),
-            dma((32,)),
-            dma((32,)),
+            dma((4,)),
         ],
         compiler_params=pltpu.CompilerParams(
             collective_id=0, has_side_effects=True, vmem_limit_bytes=28 * 2**20

time: 71.9 us -> 68.5 us (0.953)
  Pallas kernels: 69.4 us -> 66.5 us
    pallas_call x1, Pallas kernels: 69.4 us -> 66.5 us  [per_device(): pl.pallas_call(kernel, out_shape=jax.ShapeDtypeStruct((2, 2, 320, 640), j...]
where the time goes in v3:
time: 68.5 us; the launch traced here: 68.4 us
  Pallas kernels  66.5 us (97%)
  other arithmetic  1.92 us (3%)
    pallas_call x1, Pallas kernels, per_device(): pl.pallas_call(kernel, out_shape=jax.ShapeDtypeStruct((2, 2, 320, 640), j...  66.5 us
    mul x1, other arithmetic, per_device(): return sums * (1.0 / 512.0)  1.92 us

profile of v3, /device:TPU:23, one launch (start us, length us, event | category | flops | bytes accessed | tf_op | source)
XLA Modules:
  0.0 68.4 jit_solution(13355340225131078137)
XLA Ops:
  0.0 66.5 %gather_and_multiply.1 = f32[2,2,320,640]{3,2,1,0:T(8,128)S(1)} custom-call(f32[8,8,640]{2,1,0:T(8,128)} %bitcast.1), custom_call_target="tpu_custom_call" | custom-call | tf_op jit(solution)/shard_map/gather_and_multiply/pallas_call | solution.py:376
  66.5 1.9 %broadcast_multiply_fusion = f32[2,2,320,640]{3,2,1,0:T(8,128)} fusion(f32[2,2,320,640]{3,2,1,0:T(8,128)S(1)} %gather_and_multiply.1), kind=kLoop, calls=%fused_computation | loop fusion | flops 819200 | bytes 6553600 | tf_op jit(solution)/shard_map/mul | solution.py:400

commit v4 on v3

--- a/solution.py
+++ b/solution.py
@@ -6,6 +6,7 @@
 from jax.sharding import PartitionSpec as P
 
 MESH = pl.DeviceIdType.MESH
+SEGMENTS = 512
 CUT = 3
 HALF = 10
 PAD = 2
@@ -85,6 +86,13 @@
     def half(f):
         return pl.ds(HALF * f, HALF)
 
+    def both(body):
+        def one(f, carry):
+            body(f)
+            return carry
+
+        lax.fori_loop(0, 2, one, 0)
+
     def rows_copy(s, f, src, way, dev, to=None):
         to = s if to is None else to
         return remote(src.at[s + PAD, half(f)], row.at[to + PAD, half(f)], rs.at[way], rr.at[2 * to + f], dev)
@@ -119,7 +127,9 @@
     def source_start(s):
         pack(s)
         k = (s // 2) % 2
-        for f in (0, 1):
+
+        @both
+        def _(f):
             rows_copy(s, f, far, nears, ndev(k), other(s)).start()
             rows_copy(s, f, row, ups, ydev(1, k)).start()
             rows_copy(s, f, row, downs, ydev(-1, k)).start()
@@ -132,7 +142,8 @@
         return is_near | ((dy == 3) & (kind == 1))
 
     def relay(s, kind):
-        for f in (0, 1):
+        @both
+        def _(f):
             rows_wait(s, f)
 
             @pl.when(relay_up(kind))
@@ -149,11 +160,12 @@
         hi = v.astype(jnp.bfloat16)
         return hi, (v - hi.astype(jnp.float32)).astype(jnp.bfloat16)
 
-    def add(f, n, total):
+    def add(f, n, total, scale=None):
         for side in (0, 1):
             at = 256 * n + 128 * side
             p, j = at // 640, at % 640
-            out_ref[f, p, :, j : j + 128] += total[:, 128 * side : 128 * side + 128]
+            value = out_ref[f, p, :, j : j + 128] + total[:, 128 * side : 128 * side + 128]
+            out_ref[f, p, :, j : j + 128] = value if scale is None else value * scale
 
     def rhs_store(part, at, re, im):
         n = re.shape[0]
@@ -195,14 +207,14 @@
             return jnp.concatenate([hi, w - hi, hi, jnp.zeros_like(w)], axis=0).T.astype(jnp.bfloat16)
 
         for a in (0, 1):
-            w = [row[slots, HALF * f + 4 * a + 2 * p : HALF * f + 4 * a + 2 * p + 2].reshape(32, 128) for p in (0, 1)]
+            w = [row[slots, pl.ds(HALF * f + 4 * a + 2 * p, 2)].reshape(32, 128) for p in (0, 1)]
             lhs[0, pl.ds(pl.multiple_of(64 * xl + 128 * a, 64), 128)] = stacked(jnp.concatenate(w, axis=0))
-        w = row[slots, HALF * f + 8 : HALF * f + 10].reshape(32, 128)
+        w = row[slots, pl.ds(HALF * f + 8, 2)].reshape(32, 128)
         w = stacked(jnp.concatenate([w, pltpu.roll(w, 64, 1)], axis=0))
         lhs[0, pl.ds(pl.multiple_of(256 * (1 - xl), 64), 64)] = w[:64]
         col4 = col.reshape(32 + PAD, 8, 8, 640)
         (re_hi, re_lo), (im_hi, im_lo) = [
-            split(col4[slots, 4 * f + 2 * p : 4 * f + 2 * p + 2].reshape(32, 640)) for p in (0, 1)
+            split(col4[slots, pl.ds(4 * f + 2 * p, 2)].reshape(32, 640)) for p in (0, 1)
         ]
         rhs_store(0, 0, re_hi, im_hi)
         rhs_store(0, 64, re_hi, im_hi)
@@ -210,136 +222,164 @@
         rhs[0, 192:] = jnp.zeros((64, 1280), jnp.bfloat16)
         left = lhs[0]
         for n in range(5):
-            add(f, n, jnp.dot(left, rhs[0, :, 256 * n : 256 * n + 256], preferred_element_type=jnp.float32))
+            total = jnp.dot(left, rhs[0, :, 256 * n : 256 * n + 256], preferred_element_type=jnp.float32)
+            add(f, n, total, 1.0 / SEGMENTS)
 
     for d in (0, 1):
         zcopy(1, d, 0).start()
         zcopy(1, d, 1).start()
     xown(0).start()
     xown(1).start()
-    out_ref[...] = jnp.zeros_like(out_ref)
-    col[: 8 * PAD] = jnp.zeros((8 * PAD, 8, 640), jnp.float32)
-    row[:PAD] = jnp.zeros((PAD, TILES, 8, 128), jnp.float32)
+
+    def clear(i, carry):
+        out_ref[i // 20, i // 10 % 2, pl.ds(pl.multiple_of(i % 10 * 32, 32), 32)] = jnp.zeros((32, 640), jnp.float32)
+        return carry
+
+    def clear_pad(i, carry):
+        col[i] = jnp.zeros((8, 640), jnp.float32)
+        row[i // 8] = jnp.zeros((TILES, 8, 128), jnp.float32)
+        return carry
+
+    lax.fori_loop(0, 40, clear, 0)
+    lax.fori_loop(0, 8 * PAD, clear_pad, 0)
     xown(0).wait_recv()
     for d in (0, 1):
         zcopy(1, d, 2).start()
 
     def source_sends(at, kind):
-        for d in (0, 1):
+        @both
+        def _(d):
             s = 4 * at - 2 + 2 * d + kind
 
             @pl.when(is_src & (s >= 0) & (s <= 31))
             def _():
                 source_start(s)
 
-    def others_wait(s, f):
-        @pl.when((s >= 0) & (is_src_mate | (plain & ((s // 2) % 2 != core))))
-        def _():
-            rows_wait(s, f)
+    def others_wait(pair, f):
+        rows_wait(2 * pair, f)
+        rows_wait(2 * pair + 1, f)
 
     def waited(at):
         q, f = at // 2, at % 2
-        for i in range(8):
-            others_wait(8 * q + i - PAD, f)
+        for i in (0, 1):
+            theirs = 4 * q + 2 * i - 1 + core
+
+            @pl.when(plain & (theirs >= 0))
+            def _():
+                others_wait(theirs, f)
+
+        @pl.when(is_src_mate)
+        def _():
+            def wait(pair, carry):
+                others_wait(pair, f)
+                return carry
+
+            lax.fori_loop(jnp.maximum(4 * q - 1, 0), 4 * q + 3, wait, 0)
+
         compute(q, f)
 
-    def step(k, carry):
-        ring = (k >= 1) & (k <= 7)
-
-        def arrive(part):
-            for d in (1, 0):
-                zcopy(k, d, part).wait_recv()
+    def relays(turn):
+        for kind in (1, 0):
+            t = turn - turns[kind]
+            s = 2 * t - 2 * core + (flip if kind == 0 else 1 - flip)
+
+            @pl.when(plain & (t % 2 == 0) & (s >= 0) & (s <= 31))
+            def _():
+                relay(s, kind)
+
+    def arrive(k, part):
+        for d in (1, 0):
+            zcopy(k, d, part).wait_recv()
+            if d == 0 and part < 2:
+                zcopy(k + 1, d, part).start()
+            else:
 
                 @pl.when(k < 7)
                 def _():
                     zcopy(k + 1, d, part).start()
 
-                if part == 0:
-                    xcopy(k, d).start()
-                if part < 2 and d == 0:
-
-                    @pl.when(k == 7)
-                    def _():
-                        zcopy(k + 1, d, part).start()
-
-                if part == 2 and d == 1:
-
-                    @pl.when(k == 7)
-                    def _():
-                        last_a().start()
-
-        def relays(turn):
-            for kind in (1, 0):
-                t = turn - turns[kind]
-                s = 2 * t - 2 * core + (flip if kind == 0 else 1 - flip)
-
-                @pl.when(plain & (t % 2 == 0) & (s >= 0) & (s <= 31))
+            if part == 0:
+                xcopy(k, d).start()
+            if part == 2 and d == 1:
+
+                @pl.when(k == 7)
                 def _():
-                    relay(s, kind)
-
-        @pl.when(ring)
-        def _():
-            arrive(0)
+                    last_a().start()
+
+    def step(k, carry):
+        arrive(k, 0)
 
         @pl.when(k == 1)
         def _():
             xown(1).wait_recv()
 
-        @pl.when((k >= 2) & (k <= 8))
+        @pl.when(k > 1)
         def _():
             xcopy(k - 1, 1).wait_recv()
-
-            @pl.when(k == 8)
-            def _():
-                last_b().start()
-
             xcopy(k - 1, 0).wait_recv()
-
-        @pl.when(k == 9)
-        def _():
-            last_a().wait_recv()
-            last_b().wait_recv()
 
         source_sends(k - 1, 1)
         relays(2 * k)
-
-        @pl.when(ring)
-        def _():
-            arrive(1)
-
-        @pl.when(k == 8)
-        def _():
-            zcopy(k, 0, 0).wait_recv()
-            zcopy(k, 0, 1).wait_recv()
-
+        arrive(k, 1)
         source_sends(k, 0)
-
         at = k - 3 - lag
 
-        @pl.when((k <= 7) & (at >= 0))
+        @pl.when(at >= 0)
         def _():
             waited(at)
 
-        @pl.when(ring)
-        def _():
-            arrive(2)
-
+        arrive(k, 2)
         relays(2 * k + 1)
-        at = jnp.where(hops == 3, k - 4, k - jnp.where(k <= 8, 2, 3) - lag)
-        early = (k >= 7) & (k <= 8) & (at <= 5)
-        late = (k >= 9) & (at >= jnp.where(hops == 3, 5, 6)) & (at <= 7)
-
-        @pl.when(jnp.where(hops == 3, k >= 8, early | late))
+        return carry
+
+    source_sends(0, 0)
+    lax.fori_loop(1, 8, step, 0)
+    xcopy(7, 1).wait_recv()
+    last_b().start()
+
+    @pl.when(is_src)
+    def _():
+        xcopy(7, 0).wait_recv()
+        source_sends(7, 1)
+        zcopy(8, 0, 0).wait_recv()
+        zcopy(8, 0, 1).wait_recv()
+        source_sends(8, 0)
+        last_a().wait_recv()
+        last_b().wait_recv()
+        source_sends(8, 1)
+
+    def drain(k, carry):
+        @pl.when((k == 9) & jnp.logical_not(is_src))
+        def _():
+            xcopy(7, 0).wait_recv()
+
+        relays(2 * k)
+        relays(2 * k + 1)
+        at = k - 3 - lag
+
+        @pl.when(at <= 7)
         def _():
             waited(at)
 
         return carry
 
-    lax.fori_loop(0, 12, step, 0)
-    for f in (0, 1):
-        for s in (30, 31):
-            others_wait(s, f)
+    lax.fori_loop(8, 12, drain, 0)
+
+    @pl.when(jnp.logical_not(is_src))
+    def _():
+        zcopy(8, 0, 0).wait_recv()
+        zcopy(8, 0, 1).wait_recv()
+        last_a().wait_recv()
+        last_b().wait_recv()
+
+    @both
+    def _(f):
+        @pl.when(is_src_mate | (plain & (core == 0)))
+        def _():
+            others_wait(15, f)
+
         compute_last(f)
+
 
     for d in (0, 1):
         ref = col.at[pl.ds(0, 7 * (8 + CUT) + 8)]
@@ -368,6 +408,19 @@
     @pl.when(plain)
     def _():
         sent(16, mates)
+
+
+def store(sums_ref, out_ref, sems):
+    copies = [
+        pltpu.make_async_copy(sums_ref.at[f, p, h], out_ref.at[f, p, h], sems.at[4 * f + 2 * p + i])
+        for f in (0, 1)
+        for p in (0, 1)
+        for i, h in enumerate((pl.ds(0, 160), pl.ds(160, 160)))
+    ]
+    for copy in copies:
+        copy.start()
+    for copy in copies:
+        copy.wait()
 
 
 def per_device(spectra):
@@ -397,7 +450,15 @@
         ),
         name="gather_and_multiply",
     )(pltpu.with_memory_space_constraint(shard, pltpu.HBM))
-    return sums * (1.0 / 512.0)
+    return pl.pallas_call(
+        store,
+        out_shape=jax.ShapeDtypeStruct((2, 2, 320, 640), jnp.float32),
+        in_specs=[pl.BlockSpec(memory_space=pl.ANY)],
+        out_specs=pl.BlockSpec(memory_space=pl.ANY),
+        scratch_shapes=[dma((8,))],
+        compiler_params=pltpu.CompilerParams(vmem_limit_bytes=2**20),
+        name="store",
+    )(sums)
 
 
 def solution(mesh):

time: 68.5 us -> 67.6 us (0.987)
  other arithmetic: 1.92 us -> 0 us
  Pallas kernels: 66.5 us -> 67.5 us
    mul x1 -> x0, other arithmetic: 1.92 us -> none  [per_device(): return sums * (1.0 / 512.0)]
    pallas_call x0 -> x1, Pallas kernels: none -> 1.77 us  [per_device(): pl.pallas_call(store, out_shape=jax.ShapeDtypeStruct((2, 2, 320, 640), jn...]
    pallas_call x1, Pallas kernels: 66.5 us -> 65.7 us  [per_device(): pl.pallas_call(kernel, out_shape=jax.ShapeDtypeStruct((2, 2, 320, 640), j...]
where the time goes in v4:
time: 67.6 us; the launch traced here: 67.5 us
  Pallas kernels  67.5 us (100%)
    pallas_call x1, Pallas kernels, per_device(): pl.pallas_call(kernel, out_shape=jax.ShapeDtypeStruct((2, 2, 320, 640), j...  65.7 us
    pallas_call x1, Pallas kernels, per_device(): pl.pallas_call(store, out_shape=jax.ShapeDtypeStruct((2, 2, 320, 640), jn...  1.77 us

profile of v4, /device:TPU:23, one launch (start us, length us, event | category | flops | bytes accessed | tf_op | source)
XLA Modules:
  0.0 67.5 jit_solution(4645413753898570084)
XLA Ops:
  0.0 65.7 %gather_and_multiply.1.sums_ref = f32[2,2,320,640]{3,2,1,0:T(8,128)S(1)} custom-call(f32[8,8,640]{2,1,0:T(8,128)} %bitcast.1), custom_call_target="tpu_custom_call" | custom-call | tf_op jit(solution)/shard_map/gather_and_multiply/pallas_call | solution.py:429
  65.7 1.8 %store.1 = f32[2,2,320,640]{3,2,1,0:T(8,128)} custom-call(f32[2,2,320,640]{3,2,1,0:T(8,128)S(1)} %gather_and_multiply.1.sums_ref), custom_call_target="tpu_custom_call" | custom-call | tf_op jit(solution)/shard_map/store/pallas_call | solution.py:453

commit v5 on v4

--- a/solution.py
+++ b/solution.py
@@ -13,7 +13,7 @@
 TILES = 2 * HALF
 
 
-def kernel(x_ref, out_ref, col, row, far, lhs, rhs, own_sem, zs, zr, xs, xr, rr, rs):
+def kernel(x_ref, out_ref, lhs_last, rhs_last, col, row, far, lhs, rhs, own_sem, zs, zr, xs, xr, rr, rs):
     ups, downs, mates, nears = 0, 1, 2, 3
     r = lax.axis_index("row")
     c = lax.axis_index("col")
@@ -136,10 +136,10 @@
             rows_copy(s, f, row, mates, mate).start()
 
     def relay_up(kind):
-        return is_near | ((dy == 1) & (kind == 0))
+        return is_near | ((dy == 1) & (core == 1))
 
     def relay_down(kind):
-        return is_near | ((dy == 3) & (kind == 1))
+        return is_near | ((dy == 3) & (core == 0))
 
     def relay(s, kind):
         @both
@@ -160,17 +160,16 @@
         hi = v.astype(jnp.bfloat16)
         return hi, (v - hi.astype(jnp.float32)).astype(jnp.bfloat16)
 
-    def add(f, n, total, scale=None):
+    def add(f, n, total):
         for side in (0, 1):
             at = 256 * n + 128 * side
             p, j = at // 640, at % 640
-            value = out_ref[f, p, :, j : j + 128] + total[:, 128 * side : 128 * side + 128]
-            out_ref[f, p, :, j : j + 128] = value if scale is None else value * scale
-
-    def rhs_store(part, at, re, im):
+            out_ref[f, p, :, j : j + 128] += total[:, 128 * side : 128 * side + 128]
+
+    def rhs_store(ref, at, re, im):
         n = re.shape[0]
-        rhs[part, at : at + n, :640], rhs[part, at + n : at + 2 * n, :640] = re, im
-        rhs[part, at : at + n, 640:], rhs[part, at + n : at + 2 * n, 640:] = -im, re
+        ref[at : at + n, :640], ref[at + n : at + 2 * n, :640] = re, im
+        ref[at : at + n, 640:], ref[at + n : at + 2 * n, 640:] = -im, re
 
     def compute(q, f):
         slots = pl.ds(8 * q, 8)
@@ -188,8 +187,8 @@
         (re_hi, re_lo), (im_hi, im_lo) = [
             split(col4[slots, pl.ds(4 * f + 2 * p, 2)].reshape(128, 640)) for p in (0, 1)
         ]
-        rhs_store(0, 0, re_hi, im_hi)
-        rhs_store(1, 0, re_lo, im_lo)
+        rhs_store(rhs.at[0], 0, re_hi, im_hi)
+        rhs_store(rhs.at[1], 0, re_lo, im_lo)
         l_hi, l_lo = lhs[0], lhs[1]
         for n in range(5):
             lanes = slice(256 * n, 256 * n + 256)
@@ -199,31 +198,27 @@
             total += jnp.dot(l_hi, r_lo, preferred_element_type=jnp.float32)
             add(f, n, total)
 
-    def compute_last(f):
-        slots = slice(30 + PAD, 32 + PAD)
-
+    last = slice(30 + PAD, 32 + PAD)
+
+    def last_columns(f):
+        col4 = col.reshape(32 + PAD, 8, 8, 640)
+        (re_hi, re_lo), (im_hi, im_lo) = [split(col4[last, pl.ds(4 * f + 2 * p, 2)].reshape(32, 640)) for p in (0, 1)]
+        rhs_store(rhs_last.at[f], 0, re_hi, im_hi)
+        rhs_store(rhs_last.at[f], 64, re_hi, im_hi)
+        rhs_store(rhs_last.at[f], 128, re_lo, im_lo)
+        rhs_last[f, 192:] = jnp.zeros((64, 1280), jnp.bfloat16)
+
+    def last_rows(f):
         def stacked(w):
             hi = w.astype(jnp.bfloat16).astype(jnp.float32)
             return jnp.concatenate([hi, w - hi, hi, jnp.zeros_like(w)], axis=0).T.astype(jnp.bfloat16)
 
         for a in (0, 1):
-            w = [row[slots, pl.ds(HALF * f + 4 * a + 2 * p, 2)].reshape(32, 128) for p in (0, 1)]
-            lhs[0, pl.ds(pl.multiple_of(64 * xl + 128 * a, 64), 128)] = stacked(jnp.concatenate(w, axis=0))
-        w = row[slots, pl.ds(HALF * f + 8, 2)].reshape(32, 128)
+            w = [row[last, pl.ds(HALF * f + 4 * a + 2 * p, 2)].reshape(32, 128) for p in (0, 1)]
+            lhs_last[f, pl.ds(pl.multiple_of(64 * xl + 128 * a, 64), 128)] = stacked(jnp.concatenate(w, axis=0))
+        w = row[last, pl.ds(HALF * f + 8, 2)].reshape(32, 128)
         w = stacked(jnp.concatenate([w, pltpu.roll(w, 64, 1)], axis=0))
-        lhs[0, pl.ds(pl.multiple_of(256 * (1 - xl), 64), 64)] = w[:64]
-        col4 = col.reshape(32 + PAD, 8, 8, 640)
-        (re_hi, re_lo), (im_hi, im_lo) = [
-            split(col4[slots, pl.ds(4 * f + 2 * p, 2)].reshape(32, 640)) for p in (0, 1)
-        ]
-        rhs_store(0, 0, re_hi, im_hi)
-        rhs_store(0, 64, re_hi, im_hi)
-        rhs_store(0, 128, re_lo, im_lo)
-        rhs[0, 192:] = jnp.zeros((64, 1280), jnp.bfloat16)
-        left = lhs[0]
-        for n in range(5):
-            total = jnp.dot(left, rhs[0, :, 256 * n : 256 * n + 256], preferred_element_type=jnp.float32)
-            add(f, n, total, 1.0 / SEGMENTS)
+        lhs_last[f, pl.ds(pl.multiple_of(256 * (1 - xl), 64), 64)] = w[:64]
 
     for d in (0, 1):
         zcopy(1, d, 0).start()
@@ -372,14 +367,15 @@
         last_a().wait_recv()
         last_b().wait_recv()
 
+    both(last_columns)
+
     @both
     def _(f):
         @pl.when(is_src_mate | (plain & (core == 0)))
         def _():
             others_wait(15, f)
 
-        compute_last(f)
-
+        last_rows(f)
 
     for d in (0, 1):
         ref = col.at[pl.ds(0, 7 * (8 + CUT) + 8)]
@@ -397,28 +393,33 @@
         sent(16, ups)
         sent(16, downs)
 
-    @pl.when(dy == 1)
-    def _():
-        sent(8, ups)
-
-    @pl.when(dy == 3)
-    def _():
-        sent(8, downs)
+    @pl.when((dy == 1) & (core == 1))
+    def _():
+        sent(16, ups)
+
+    @pl.when((dy == 3) & (core == 0))
+    def _():
+        sent(16, downs)
 
     @pl.when(plain)
     def _():
         sent(16, mates)
 
 
-def store(sums_ref, out_ref, sems):
-    copies = [
-        pltpu.make_async_copy(sums_ref.at[f, p, h], out_ref.at[f, p, h], sems.at[4 * f + 2 * p + i])
-        for f in (0, 1)
-        for p in (0, 1)
-        for i, h in enumerate((pl.ds(0, 160), pl.ds(160, 160)))
-    ]
-    for copy in copies:
-        copy.start()
+def finish(sums_ref, lhs_ref, rhs_ref, out_ref, buf, sems):
+    copies = []
+    for f in (0, 1):
+        left = lhs_ref[f]
+        for n in range(5):
+            total = jnp.dot(left, rhs_ref[f, :, 256 * n : 256 * n + 256], preferred_element_type=jnp.float32)
+            for side in (0, 1):
+                at = 256 * n + 128 * side
+                p, j = at // 640, at % 640
+                value = sums_ref[f, p, :, j : j + 128] + total[:, 128 * side : 128 * side + 128]
+                buf[f, p, :, j : j + 128] = value * (1.0 / SEGMENTS)
+                if j == 512:
+                    copies.append(pltpu.make_async_copy(buf.at[f, p], out_ref.at[f, p], sems.at[2 * f + p]))
+                    copies[-1].start()
     for copy in copies:
         copy.wait()
 
@@ -426,11 +427,15 @@
 def per_device(spectra):
     shard = spectra.reshape(8, 8, 640)
     dma = pltpu.SemaphoreType.DMA
-    sums = pl.pallas_call(
+    parts = pl.pallas_call(
         kernel,
-        out_shape=jax.ShapeDtypeStruct((2, 2, 320, 640), jnp.float32),
+        out_shape=(
+            jax.ShapeDtypeStruct((2, 2, 320, 640), jnp.float32),
+            jax.ShapeDtypeStruct((2, 320, 256), jnp.bfloat16),
+            jax.ShapeDtypeStruct((2, 256, 1280), jnp.bfloat16),
+        ),
         in_specs=[pl.BlockSpec(memory_space=pltpu.HBM)],
-        out_specs=pl.BlockSpec(memory_space=pltpu.VMEM),
+        out_specs=(pl.BlockSpec(memory_space=pltpu.VMEM),) * 3,
         scratch_shapes=[
             pltpu.VMEM((8 * (32 + PAD), 8, 640), jnp.float32),
             pltpu.VMEM((32 + PAD, TILES, 8, 128), jnp.float32),
@@ -451,14 +456,14 @@
         name="gather_and_multiply",
     )(pltpu.with_memory_space_constraint(shard, pltpu.HBM))
     return pl.pallas_call(
-        store,
+        finish,
         out_shape=jax.ShapeDtypeStruct((2, 2, 320, 640), jnp.float32),
-        in_specs=[pl.BlockSpec(memory_space=pl.ANY)],
+        in_specs=[pl.BlockSpec(memory_space=pltpu.VMEM)] * 3,
         out_specs=pl.BlockSpec(memory_space=pl.ANY),
-        scratch_shapes=[dma((8,))],
-        compiler_params=pltpu.CompilerParams(vmem_limit_bytes=2**20),
-        name="store",
-    )(sums)
+        scratch_shapes=[pltpu.VMEM((2, 2, 320, 640), jnp.float32), dma((4,))],
+        compiler_params=pltpu.CompilerParams(vmem_limit_bytes=16 * 2**20),
+        name="finish",
+    )(*parts)
 
 
 def solution(mesh):

time: 67.6 us -> 67.4 us (level)
  no operation moved by 1% of the time
where the time goes in v5:
time: 67.4 us; the launch traced here: 67.3 us
  Pallas kernels  67.2 us (100%)
    pallas_call x1, Pallas kernels, per_device(): pl.pallas_call(kernel, out_shape=(jax.ShapeDtypeStruct((2, 2, 320, 640),...  65.2 us
    pallas_call x1, Pallas kernels, per_device(): pl.pallas_call(finish, out_shape=jax.ShapeDtypeStruct((2, 2, 320, 640), j...  2.08 us

profile of v5, /device:TPU:23, one launch (start us, length us, event | category | flops | bytes accessed | tf_op | source)
XLA Modules:
  0.0 67.3 jit_solution(9121179644601206087)
XLA Ops:
  0.0 65.2 %gather_and_multiply.1 = (f32[2,2,320,640]{3,2,1,0:T(8,128)S(1)}, bf16[2,320,256]{2,1,0:T(8,128)(2,1)S(1)}, bf16[2,256,1280]{2,1,0:T(8,128)(2,1)S(1)}) custom-call(f32[8,8,640]{2,1,0:T(8,128)} %bitcast.1), custom_call_target="tpu_custom_call" | custom-call | tf_op jit(solution)/shard_map/gather_and_multiply/pallas_call | solution.py:430
  65.2 2.1 %finish.1 = f32[2,2,320,640]{3,2,1,0:T(8,128)} custom-call(f32[2,2,320,640]{3,2,1,0:T(8,128)S(1)} %get-tuple-element.8.sums_ref, bf16[2,320,256]{2,1,0:T(8,128)(2,1)S(1)} %get-tuple-element.9.lhs_ref, bf16[2,256,1280]{2,1,0:T(8,128)(2,1)S(1)} %get-tuple-element.10.rhs_ref), custom_call_target="tpu_custom_call" | custom-call | tf_op jit(solution)/shard_map/finish/pallas_call | solution.py:458

commit v6 on v5

--- a/solution.py
+++ b/solution.py
@@ -29,6 +29,8 @@
     hops = jnp.where(home, 0, 1) + jnp.where(dy == 0, 0, 1) + jnp.where(dy == 2, 1, 0)
     lag = jnp.where(hops >= 2, 1, 0)
     turns = (hops + 1 + jnp.where(hops == 3, 1, 0), 2 * hops + jnp.where(hops == 3, 0, 1))
+    passes = plain & (core == 1)
+    takes = is_src_mate | (plain & (core == 0))
     flip = jnp.where(home, 0, 1)
 
     zdev = [((r + 2) % 32, c), ((r + 30) % 32, c)]
@@ -126,33 +128,32 @@
 
     def source_start(s):
         pack(s)
-        k = (s // 2) % 2
 
         @both
         def _(f):
-            rows_copy(s, f, far, nears, ndev(k), other(s)).start()
-            rows_copy(s, f, row, ups, ydev(1, k)).start()
-            rows_copy(s, f, row, downs, ydev(-1, k)).start()
+            rows_copy(s, f, far, nears, ndev(1), other(s)).start()
+            rows_copy(s, f, row, ups, ydev(1, 1)).start()
+            rows_copy(s, f, row, downs, ydev(-1, 1)).start()
             rows_copy(s, f, row, mates, mate).start()
 
-    def relay_up(kind):
-        return is_near | ((dy == 1) & (core == 1))
-
-    def relay_down(kind):
-        return is_near | ((dy == 3) & (core == 0))
-
-    def relay(s, kind):
+    def relay_up(d):
+        return is_near | (dy == 1) if d == 0 else is_near
+
+    def relay_down(d):
+        return is_near | (dy == 3) if d == 1 else is_near
+
+    def relay(s, d):
         @both
         def _(f):
             rows_wait(s, f)
 
-            @pl.when(relay_up(kind))
+            @pl.when(relay_up(d))
             def _():
-                rows_copy(s, f, row, ups, ydev(1, core)).start()
-
-            @pl.when(relay_down(kind))
+                rows_copy(s, f, row, ups, ydev(1, 1)).start()
+
+            @pl.when(relay_down(d))
             def _():
-                rows_copy(s, f, row, downs, ydev(-1, core)).start()
+                rows_copy(s, f, row, downs, ydev(-1, 1)).start()
 
             rows_copy(s, f, row, mates, mate).start()
 
@@ -256,14 +257,8 @@
 
     def waited(at):
         q, f = at // 2, at % 2
-        for i in (0, 1):
-            theirs = 4 * q + 2 * i - 1 + core
-
-            @pl.when(plain & (theirs >= 0))
-            def _():
-                others_wait(theirs, f)
-
-        @pl.when(is_src_mate)
+
+        @pl.when(takes)
         def _():
             def wait(pair, carry):
                 others_wait(pair, f)
@@ -276,11 +271,15 @@
     def relays(turn):
         for kind in (1, 0):
             t = turn - turns[kind]
-            s = 2 * t - 2 * core + (flip if kind == 0 else 1 - flip)
-
-            @pl.when(plain & (t % 2 == 0) & (s >= 0) & (s <= 31))
+
+            @pl.when(passes & (t % 2 == 0))
             def _():
-                relay(s, kind)
+                for d in (0, 1):
+                    s = 2 * t - 2 + 2 * d + (flip if kind == 0 else 1 - flip)
+
+                    @pl.when((s >= 0) & (s <= 31))
+                    def _():
+                        relay(s, d)
 
     def arrive(k, part):
         for d in (1, 0):
@@ -371,7 +370,7 @@
 
     @both
     def _(f):
-        @pl.when(is_src_mate | (plain & (core == 0)))
+        @pl.when(takes)
         def _():
             others_wait(15, f)
 
@@ -388,22 +387,22 @@
         for way in (ups, downs, mates, nears):
             sent(32, way)
 
-    @pl.when(is_near)
+    @pl.when(passes)
+    def _():
+        sent(32, mates)
+
+    @pl.when(passes & is_near)
+    def _():
+        sent(32, ups)
+        sent(32, downs)
+
+    @pl.when(passes & (dy == 1))
     def _():
         sent(16, ups)
+
+    @pl.when(passes & (dy == 3))
+    def _():
         sent(16, downs)
-
-    @pl.when((dy == 1) & (core == 1))
-    def _():
-        sent(16, ups)
-
-    @pl.when((dy == 3) & (core == 0))
-    def _():
-        sent(16, downs)
-
-    @pl.when(plain)
-    def _():
-        sent(16, mates)
 
 
 def finish(sums_ref, lhs_ref, rhs_ref, out_ref, buf, sems):

time: 67.4 us -> 65.3 us (0.969)
  Pallas kernels: 67.2 us -> 65.2 us
    pallas_call x1, Pallas kernels: 65.2 us -> 63.1 us  [per_device(): pl.pallas_call(kernel, out_shape=(jax.ShapeDtypeStruct((2, 2, 320, 640),...]
where the time goes in v6:
time: 65.3 us; the launch traced here: 65.2 us
  Pallas kernels  65.2 us (100%)
    pallas_call x1, Pallas kernels, per_device(): pl.pallas_call(kernel, out_shape=(jax.ShapeDtypeStruct((2, 2, 320, 640),...  63.1 us
    pallas_call x1, Pallas kernels, per_device(): pl.pallas_call(finish, out_shape=jax.ShapeDtypeStruct((2, 2, 320, 640), j...  2.08 us

profile of v6, /device:TPU:23, one launch (start us, length us, event | category | flops | bytes accessed | tf_op | source)
XLA Modules:
  0.0 65.2 jit_solution(11369423898282937156)
XLA Ops:
  0.0 63.1 %gather_and_multiply.1 = (f32[2,2,320,640]{3,2,1,0:T(8,128)S(1)}, bf16[2,320,256]{2,1,0:T(8,128)(2,1)S(1)}, bf16[2,256,1280]{2,1,0:T(8,128)(2,1)S(1)}) custom-call(f32[8,8,640]{2,1,0:T(8,128)} %bitcast.1), custom_call_target="tpu_custom_call" | custom-call | tf_op jit(solution)/shard_map/gather_and_multiply/pallas_call | solution.py:429
  63.1 2.1 %finish.1 = f32[2,2,320,640]{3,2,1,0:T(8,128)} custom-call(f32[2,2,320,640]{3,2,1,0:T(8,128)S(1)} %get-tuple-element.8.sums_ref, bf16[2,320,256]{2,1,0:T(8,128)(2,1)S(1)} %get-tuple-element.9.lhs_ref, bf16[2,256,1280]{2,1,0:T(8,128)(2,1)S(1)} %get-tuple-element.10.rhs_ref), custom_call_target="tpu_custom_call" | custom-call | tf_op jit(solution)/shard_map/finish/pallas_call | solution.py:457

commit v7 on v6

--- a/solution.py
+++ b/solution.py
@@ -49,12 +49,16 @@
     own = pltpu.make_async_copy(x_ref, col.at[blk(0, slice(0, 8))], own_sem)
     own.start()
     barrier = pltpu.get_barrier_semaphore()
-    greet = [zdev[0], zdev[1], xdev, mate]
-    greet += [ydev(s, k) for s in (1, -1) for k in (0, 1)] + [ndev(0), ndev(1)]
-    for d in greet:
+    for d in [zdev[0], zdev[1], xdev, mate]:
         pl.semaphore_signal(barrier, inc=1, device_id=d, device_id_type=MESH)
+
+    @pl.when(core == 1)
+    def _():
+        for d in [ydev(s, k) for s in (1, -1) for k in (0, 1)] + [ndev(0), ndev(1)]:
+            pl.semaphore_signal(barrier, inc=1, device_id=d, device_id_type=MESH)
+
     own.wait()
-    pl.semaphore_wait(barrier, len(greet))
+    pl.semaphore_wait(barrier, 7)
 
     A, B = slice(0, CUT), slice(CUT, 8)
 
@@ -302,6 +306,7 @@
 
     def step(k, carry):
         arrive(k, 0)
+        relays(2 * k)
 
         @pl.when(k == 1)
         def _():
@@ -313,7 +318,6 @@
             xcopy(k - 1, 0).wait_recv()
 
         source_sends(k - 1, 1)
-        relays(2 * k)
         arrive(k, 1)
         source_sends(k, 0)
         at = k - 3 - lag

time: 65.3 us -> 64.7 us (level)
  Pallas kernels: 65.2 us -> 64.5 us
    pallas_call x1, Pallas kernels: 63.1 us -> 62.4 us  [per_device(): pl.pallas_call(kernel, out_shape=(jax.ShapeDtypeStruct((2, 2, 320, 640),...]
where the time goes in v7:
time: 64.7 us; the launch traced here: 64.5 us
  Pallas kernels  64.5 us (100%)
    pallas_call x1, Pallas kernels, per_device(): pl.pallas_call(kernel, out_shape=(jax.ShapeDtypeStruct((2, 2, 320, 640),...  62.4 us
    pallas_call x1, Pallas kernels, per_device(): pl.pallas_call(finish, out_shape=jax.ShapeDtypeStruct((2, 2, 320, 640), j...  2.08 us

profile of v7, /device:TPU:23, one launch (start us, length us, event | category | flops | bytes accessed | tf_op | source)
XLA Modules:
  0.0 64.5 jit_solution(10904542206508271363)
XLA Ops:
  0.0 62.4 %gather_and_multiply.1 = (f32[2,2,320,640]{3,2,1,0:T(8,128)S(1)}, bf16[2,320,256]{2,1,0:T(8,128)(2,1)S(1)}, bf16[2,256,1280]{2,1,0:T(8,128)(2,1)S(1)}) custom-call(f32[8,8,640]{2,1,0:T(8,128)} %bitcast.1), custom_call_target="tpu_custom_call" | custom-call | tf_op jit(solution)/shard_map/gather_and_multiply/pallas_call | solution.py:433
  62.5 2.1 %finish.1 = f32[2,2,320,640]{3,2,1,0:T(8,128)} custom-call(f32[2,2,320,640]{3,2,1,0:T(8,128)S(1)} %get-tuple-element.8.sums_ref, bf16[2,320,256]{2,1,0:T(8,128)(2,1)S(1)} %get-tuple-element.9.lhs_ref, bf16[2,256,1280]{2,1,0:T(8,128)(2,1)S(1)} %get-tuple-element.10.rhs_ref), custom_call_target="tpu_custom_call" | custom-call | tf_op jit(solution)/shard_map/finish/pallas_call | solution.py:461
